TPU v7x, 32 devices: a whole 2x2x4 slice. The times are simulated.
32 devices in a mesh: groups: 2 (over y), tm: 8 (over z, x), space: 2 (over core).
Axes of the slice: x: 2, y: 2, z: 4, core: 2. Of those that a mesh axis runs over, the one named last changes fastest.
Arguments:
- interior_diag: bfloat16 [24576, 1536], P(('groups', 'tm'), 'space'), parts along dimension 0, may hold values from -1 to 5, as said below
- coupling: bfloat16 [24576, 1536], P(('groups', 'tm'), 'space'), parts along dimension 0, may hold values from -0.29882812 to 0.29882812
- arrow_rows: bfloat16 [12288, 1536], P(('groups', 'tm', 'space')), parts along dimension 0, may hold values from -0.59765625 to 0.59765625
- separator_diag: bfloat16 [24576, 1536], P(('groups', 'tm'), 'space'), parts along dimension 0, may hold values from -1 to 5, as said below
- tip: bfloat16 [1536, 768], P('groups', 'space'), parts along dimension 0, may hold values from -6 to 6
- lengths: int32 [16], P('groups'), parts along dimension 0, may hold values from 1 to 2, 12 in all
Outputs:
- new_separator: bfloat16 [24576, 1536], P(('groups', 'tm'), 'space'), parts along dimension 0
- arrow_fill: bfloat16 [12288, 1536], P(('groups', 'tm'), 'space'), parts along dimension 0
- new_tip: float32 [1536, 768], P('groups', 'space'), parts along dimension 0
There are 2 independent parts, one for each index of `groups`. A program takes and returns all parts, laid end to end along the dimension named above; each array names one. Nothing has to cross between parts.
Inputs may be any that keep to these rules, and one draw needn't show every extreme that they name: `interior_diag`: each block of 1536 rows is symmetric with eigenvalues above 0.5. `separator_diag`: each block of 1536 rows is symmetric with eigenvalues above 0.5. `lengths`: partition p has an interior block exactly when entry p is 2; some entry is 2.
All inputs are finite; a program needn't handle non-finite values.
Results may differ from a plain program's by a relative error of at most 0.008.
Values may be sent and summed in bfloat16 or wider, within the bound.
A program may use at most 128 MiB of HBM per device.

v0:
```python
import jax
import jax.numpy as jnp
from jax import lax
from jax.sharding import PartitionSpec as P


def shifted(block, axis, distance):
    devices = range(lax.axis_size(axis))
    route = [(i - distance, i) for i in devices if i - distance in devices]
    return lax.ppermute(block, axis, route)


def solve_block(operands):
    whole_diag, right_sides = operands
    factor = jnp.linalg.cholesky(whole_diag.astype(jnp.float32))
    solved = lax.linalg.triangular_solve(factor, right_sides, left_side=True, lower=True)
    return solved.astype(jnp.bfloat16)


def skip_block(operands):
    return jnp.zeros(operands[1].shape, jnp.bfloat16)


def gram_terms(local_e, local_r, full_e, full_r):
    boundary = jnp.einsum("kb,kc->bc", full_e, local_e, preferred_element_type=jnp.float32)
    arrow_term = -jnp.einsum("ka,kc->ac", full_r, local_e, preferred_element_type=jnp.float32)
    tip_term = jnp.einsum("ka,kc->ac", full_r, local_r, preferred_element_type=jnp.float32)
    return (boundary, arrow_term, tip_term)


def on_device(interior_diag, coupling, arrow_rows, separator_diag, tip, lengths):
    position = lax.axis_index("tm")
    whole_diag = lax.all_gather(interior_diag, "space", axis=1, tiled=True)
    couple = jnp.where(
        position == 0, jnp.zeros(coupling.shape, jnp.float32), coupling.astype(jnp.float32)
    )
    right_sides = jnp.concatenate([couple, arrow_rows.astype(jnp.float32).T], axis=1)
    solved = lax.cond(lengths[position] == 2, solve_block, skip_block, (whole_diag, right_sides))
    split_at = coupling.shape[1]
    solved_e = solved[:, :split_at]
    solved_r = solved[:, split_at:]
    full_e, full_r = (
        lax.all_gather(solved_e, "space", axis=1, tiled=True),
        lax.all_gather(solved_r, "space", axis=1, tiled=True),
    )
    own_boundary, own_arrow, tip_term = gram_terms(solved_e, solved_r, full_e, full_r)
    boundary, arrow_term = (
        shifted(own_boundary.astype(jnp.bfloat16), "tm", -1).astype(own_boundary.dtype),
        shifted(own_arrow.astype(jnp.bfloat16), "tm", -1).astype(own_arrow.dtype),
    )
    tip_sum = lax.psum(tip_term, "tm")
    new_separator = (separator_diag.astype(jnp.float32) - boundary).astype(jnp.bfloat16)
    arrow_fill = arrow_term.astype(jnp.bfloat16)
    new_tip = tip.astype(jnp.float32) - tip_sum
    return (new_separator, arrow_fill, new_tip)


def solution(mesh):
    return jax.shard_map(
        on_device,
        mesh=mesh,
        in_specs=(
            P(("groups", "tm"), "space"),
            P(("groups", "tm"), "space"),
            P(("groups", "tm", "space"), None),
            P(("groups", "tm"), "space"),
            P("groups", "space"),
            P("groups"),
        ),
        out_specs=(
            P(("groups", "tm"), "space"),
            P(("groups", "tm"), "space"),
            P("groups", "space"),
        ),
        check_vma=False,
    )
```

profile of v0, /device:TPU:0, one launch (start us, length us, event | category | flops | bytes accessed | tf_op | source)
XLA Modules:
  0.0 753.0 jit_solution(16959039590199591219)
XLA Ops:
  7.2 0.0 copy-start.6
  7.2 0.0 all-gather.4.cloned.1.call-start
  7.2 4.3 copy.10
  11.5 0.0 copy-start.1
  11.5 0.0 all-gather.4.cloned.1.call-update
  11.5 0.0 all-gather.6.cloned.1.call-start
  11.6 0.0 copy-done.6
  11.6 0.6 dynamic_slice.3
  12.9 1.7 copy.11
  14.6 0.2 convert_bitcast_fusion
  14.7 0.0 copy-done.1
  14.7 0.3 convert_select_fusion
  15.1 3.3 pad_maximum_fusion
  18.4 10.4 %all-gather.4.cloned.1.call-done = bf16[1536,1536]{0,1:T(8,128)(2,1)} async-done(((bf16[1536,768]{0,1:T(8,128)(2,1)}), bf16[1536,1536]{0,1:T(8,128)(2,1)}) %all-gather.4.cloned.1.call-update) | async-done | bytes 4718608 | tf_op jit(solution)/shard_map/all_gather | solution.py:33
  28.8 2.7 conditional.1
  28.8 1.1 slice.446
  29.9 1.6 slice.445
  31.5 0.0 all-gather.6.cloned.1.call-update
  31.5 0.0 all-gather.8.cloned.1.call-start
  31.6 0.7 all-gather.8.cloned.1.call-update
  32.3 0.0 all-reduce.3.cloned.1.call-start
  32.3 580.0 %all-gather.6.cloned.1.call-done = bf16[1536,1536]{1,0:T(8,128)(2,1)} async-done(((bf16[1536,768]{1,0:T(8,128)(2,1)}), bf16[1536,1536]{1,0:T(8,128)(2,1)}) %all-gather.6.cloned.1.call-update) | async-done | bytes 4718608 | tf_op jit(solution)/shard_map/all_gather | solution.py:43
  612.3 8.4 %convolution_convert_fusion.1 = bf16[1536,768]{1,0:T(8,128)(2,1)} fusion(bf16[1536,1536]{1,0:T(8,128)(2,1)} %all-gather.6.cloned.1.call-done, bf16[1536,768]{1,0:T(8,128)(2,1)} %get-tuple-element.20), kind=kOutput, calls=%fused_computation.263 | convolution fusion | flops 3625058304 | bytes 9437184 | tf_op jit(solution)/shard_map/kb,kc->bc/dot_general | solution.py:25
  620.8 1.3 collective-permute-start
  622.1 4.5 all-gather.8.cloned.1.call-done
  626.5 0.0 copy-start.5
  626.6 5.6 negate_convert_fusion
  632.1 0.0 copy-start.2
  632.1 1.4 collective-permute-start.1
  633.6 0.0 copy-done.5
  633.6 3.7 fusion.115
  637.3 0.0 all-reduce.3.cloned.1.call-update
  637.3 72.7 %collective-permute-done.1 = bf16[768,768]{1,0:T(8,128)(2,1)S(1)} collective-permute-done((bf16[768,768]{1,0:T(8,128)(2,1)}, bf16[768,768]{1,0:T(8,128)(2,1)S(1)}, u32[]{:S(2)}, u32[]{:S(2)}) %collective-permute-start.1) | collective-permute-done | bytes 1179680 | tf_op jit(solution)/shard_map/ppermute | solution.py:10
  710.0 29.2 %all-reduce.3.cloned.1.call-done = f32[768,384]{1,0:T(8,128)} async-done(((f32[768,384]{1,0:T(8,128)}), f32[768,384]{1,0:T(8,128)}) %all-reduce.3.cloned.1.call-update) | async-done | bytes 1179664 | tf_op jit(solution)/shard_map/psum | solution.py:51
  739.2 2.5 convert_subtract_fusion
  741.8 0.0 collective-permute-done
  741.8 0.0 copy-done.2
  741.8 3.7 subtract_convert_fusion
  745.4 1.0 copy.109
Async XLA Ops:
  7.2 4.4 copy-start.6
  7.2 21.6 %all-gather.4.cloned.1.call-start = ((), (), s32[]{:S(2)}) async-start(), calls=%async_computation | async-start | bytes 7077888 | tf_op jit(solution)/shard_map/all_gather | solution.py:33
  11.5 3.2 copy-start.1
  11.5 600.8 %all-gather.6.cloned.1.call-start = ((), (), s32[]{:S(2)}) async-start(), calls=%async_computation.1 | async-start | bytes 7077888 | tf_op jit(solution)/shard_map/all_gather | solution.py:43
  31.5 595.0 %all-gather.8.cloned.1.call-start = ((), (), s32[]{:S(2)}) async-start(), calls=%async_computation.2 | async-start | bytes 3538944 | tf_op jit(solution)/shard_map/all_gather | solution.py:44
  32.3 707.0 %all-reduce.3.cloned.1.call-start = ((), (), s32[]{:S(2)}) async-start(), calls=%async_computation.3 | async-start | bytes 2359296 | tf_op jit(solution)/shard_map/psum | solution.py:51
  620.8 121.0 %collective-permute-start = (bf16[1536,768]{1,0:T(8,128)(2,1)}, bf16[1536,768]{1,0:T(8,128)(2,1)}, u32[]{:S(2)}, u32[]{:S(2)}) collective-permute-start(bf16[1536,768]{1,0:T(8,128)(2,1)} %convolution_convert_fusion.1), channel_id=1, source_target_pairs={{2,0},{4,2},{6,4},{8,6},{10,8},{12,10},{14,12},{3,1},{5,3},{7,5},{... | collective-permute-start | bytes 7077896 | tf_op jit(solution)/shard_map/ppermute | solution.py:10
  626.5 7.0 copy-start.5
  632.1 109.6 %copy-start.2 = (bf16[1536,768]{1,0:T(8,128)(2,1)S(1)}, bf16[1536,768]{1,0:T(8,128)(2,1)}, u32[]{:S(2)}) copy-start(bf16[1536,768]{1,0:T(8,128)(2,1)} %param.11) | copy-start | bytes 7077892
  632.1 77.9 %collective-permute-start.1 = (bf16[768,768]{1,0:T(8,128)(2,1)}, bf16[768,768]{1,0:T(8,128)(2,1)S(1)}, u32[]{:S(2)}, u32[]{:S(2)}) collective-permute-start(bf16[768,768]{1,0:T(8,128)(2,1)} %negate_convert_fusion), channel_id=1, source_target_pairs={{2,0},{4,2},{6,4},{8,6},{10,8},{12,10},{14,12},{3,1},{5,3},{7,5},{... | collective-permute-start | bytes 3538952 | tf_op jit(solution)/shard_map/ppermute | solution.py:10
Sparse Core Ops, SparseCore 0:
  11.6 17.1 all-gather.3
  31.6 580.6 all-gather.5
  614.4 12.0 all-gather.7
  637.4 101.7 all-reduce.2
where the time goes:
time: 758 us; the launch traced here: 753 us
  waiting for transfers between devices  698 us (92%)
  matrix products  17.7 us (2%)
  between operations  14.5 us (2%)
  local copies, waits for them, and re-layouts  10.3 us (1%)
  other arithmetic  10 us (1%)
    all_gather x1, waiting for transfers between devices, on_device(): lax.all_gather(solved_e, 'space', axis=1, tiled=True)  580 us
    ppermute x2, waiting for transfers between devices, shifted(): return lax.ppermute(block, axis, route)  72.7 us
    psum x1, waiting for transfers between devices, on_device(): tip_sum = lax.psum(tip_term, 'tm')  29.2 us
  transfers between devices with their start and end apart: 6, of which 5 were waited for; matrix products, arithmetic and copies ran while one was open for 4% of the time, Pallas kernels for 0%

commit v1 on v0

v1 whole, which is shorter than its diff:
```python
import functools

import jax
import jax.numpy as jnp
from jax import lax
from jax.experimental import pallas as pl
from jax.experimental.pallas import tpu as pltpu
from jax.sharding import PartitionSpec as P

BLOCK = 256
VMEM_LIMIT = 50 * 1024 * 1024


def shifted(block, axis, distance):
    devices = range(lax.axis_size(axis))
    route = [(i - distance, i) for i in devices if i - distance in devices]
    return lax.ppermute(block, axis, route)


def low(x):
    return x.astype(jnp.bfloat16)


def product(a, b):
    return jnp.dot(a, b, preferred_element_type=jnp.float32)


def invert(s, x_ref):
    size = s.shape[0]
    eye = lax.broadcasted_iota(jnp.int32, s.shape, 0) == lax.broadcasted_iota(jnp.int32, s.shape, 1)
    unit = eye.astype(jnp.float32)
    diagonal = jnp.where(eye, s, 0.0)
    row_scale = lax.rsqrt(jnp.sum(diagonal, axis=1, keepdims=True))
    column_scale = lax.rsqrt(jnp.sum(diagonal, axis=0, keepdims=True))
    a = s * row_scale * column_scale
    bound = jnp.max(jnp.sum(jnp.abs(a), axis=0, keepdims=True), axis=1, keepdims=True)
    step = 1.5 / bound
    e = unit - step * a
    e1 = low(e)
    e2 = low(product(e1, e1))
    e4 = low(product(e2, e2))
    x = unit + e
    x = x + product(low(x), e2)
    x = x + product(low(x), e4)
    x_ref[...] = step * x
    a_low = low(a)

    def unfinished(state):
        count, error = state
        return jnp.logical_and(error > 0.01, count < 24)

    def refine(state):
        count, _ = state
        x_low = low(x_ref[...])
        residual = unit - product(a_low, x_low)
        x_ref[...] = x_low.astype(jnp.float32) + product(x_low, low(residual))
        return count + 1, jnp.sum(residual * residual)

    lax.while_loop(unfinished, refine, (jnp.int32(0), jnp.float32(1.0)))
    return x_ref[...] * row_scale * column_scale


def factor_kernel(active_ref, halves_ref, lt_ref, p_ref, d_ref, u_ref, x_ref):
    n = d_ref.shape[0]
    width = halves_ref.shape[1]
    for half in range(n // width):
        d_ref[:, half * width:(half + 1) * width] = halves_ref[half * n:(half + 1) * n, :]
    keep = active_ref[0] == 2
    for k in range(n // BLOCK):
        lo, hi = k * BLOCK, (k + 1) * BLOCK
        row = d_ref[lo:hi, lo:].astype(jnp.float32)
        if k:
            row = row - product(lt_ref[lo:hi, :lo], u_ref[:lo, lo:])
        p = invert(row[:, :BLOCK], x_ref)
        p_low = low(p)
        p_ref[lo:hi, :] = low(jnp.where(keep, p, 0.0))
        lt_ref[lo:hi, lo:hi] = p_low
        if hi < n:
            row_low = low(row[:, BLOCK:])
            u_ref[lo:hi, hi:] = row_low
            lt_ref[lo:hi, hi:] = low(product(p_low, row_low))
            column = d_ref[hi:, lo:hi].astype(jnp.float32)
            if k:
                column = column - product(lt_ref[hi:, :lo], u_ref[:lo, lo:hi])
            lt_ref[hi:, lo:hi] = low(product(low(column), p_low))


def solve_kernel(lt_ref, p_ref, e_ref, r_ref, we_ref, ze_ref, wr_ref, zr_ref, arrow_ref):
    n = lt_ref.shape[0]
    for k in range(n // BLOCK):
        lo, hi = k * BLOCK, (k + 1) * BLOCK
        e = e_ref[lo:hi, :]
        r = r_ref[:, lo:hi]
        if k:
            e = low(e.astype(jnp.float32) - product(lt_ref[lo:hi, :lo], we_ref[:lo, :]))
            r = low(r.astype(jnp.float32) - product(wr_ref[:, :lo], lt_ref[:lo, lo:hi]))
        we_ref[lo:hi, :] = e
        wr_ref[:, lo:hi] = r
        ze_ref[lo:hi, :] = low(product(p_ref[lo:hi, :], e))
        zr_ref[:, lo:hi] = low(product(r, p_ref[lo:hi, :]))
    arrow_ref[...] = low(-product(wr_ref[...], ze_ref[...]))


def in_vmem(count):
    return [pl.BlockSpec(memory_space=pltpu.VMEM)] * count


def shape_of(*dims):
    return jax.ShapeDtypeStruct(dims, jnp.bfloat16)


def factored(length, halves):
    width = halves.shape[1]
    n = halves.shape[0] * width // (halves.shape[0] // 2)
    return pl.pallas_call(
        factor_kernel,
        out_shape=(shape_of(n, n), shape_of(n, BLOCK)),
        in_specs=[pl.BlockSpec(memory_space=pltpu.SMEM)] + in_vmem(1),
        out_specs=tuple(in_vmem(2)),
        scratch_shapes=[
            pltpu.VMEM((n, n), jnp.bfloat16),
            pltpu.VMEM((n, n), jnp.bfloat16),
            pltpu.VMEM((BLOCK, BLOCK), jnp.float32),
        ],
        compiler_params=pltpu.CompilerParams(vmem_limit_bytes=VMEM_LIMIT),
        cost_estimate=pl.CostEstimate(flops=n * n * n, bytes_accessed=4 * n * n, transcendentals=0),
        name="factor",
    )(length, halves)


def eliminated(lt, p, couple, arrows):
    n, columns = couple.shape
    rows = arrows.shape[0]
    return pl.pallas_call(
        solve_kernel,
        out_shape=(
            shape_of(n, columns), shape_of(n, columns),
            shape_of(rows, n), shape_of(rows, n), shape_of(rows, columns),
        ),
        in_specs=in_vmem(4),
        out_specs=tuple(in_vmem(5)),
        compiler_params=pltpu.CompilerParams(vmem_limit_bytes=VMEM_LIMIT),
        cost_estimate=pl.CostEstimate(
            flops=n * n * (columns + rows) + 2 * n * columns * rows,
            bytes_accessed=2 * (n * n + 3 * n * columns + 3 * n * rows),
            transcendentals=0,
        ),
        name="solve",
    )(lt, p, couple, arrows)


def on_device(interior_diag, coupling, arrow_rows, separator_diag, tip, lengths):
    position = lax.axis_index("tm")
    core = lax.axis_index("space")
    halves = lax.all_gather(interior_diag, "space", axis=0, tiled=True)
    arrows = lax.all_gather(arrow_rows, "space", axis=0, tiled=True)
    length = lax.dynamic_slice(lengths, (position,), (1,))
    lt, p = factored(length, halves)
    we, ze, wr, zr, own_arrow = eliminated(lt, p, coupling, arrows)
    arrow_fill = shifted(own_arrow, "tm", -1)

    other_ze = lax.ppermute(ze, "space", [(0, 1), (1, 0)])
    first = core == 0
    width = coupling.shape[1]
    part = width // 2
    left = jnp.where(first, we[:, :part], other_ze[:, part:])
    right = jnp.where(first, other_ze, we)
    cross = low(jnp.einsum("kb,kc->bc", left, right, preferred_element_type=jnp.float32))
    cross = shifted(cross, "tm", -1)
    own = low(jnp.einsum("kb,kc->bc", we, ze, preferred_element_type=jnp.float32))
    own = shifted(own, "tm", -1)
    cross = lax.all_gather(cross, "space", axis=0, tiled=True)

    tip_width = tip.shape[1]
    zr_own = lax.dynamic_slice(zr, (core * tip_width, 0), (tip_width, zr.shape[1]))
    tip_term = jnp.einsum("ak,ck->ac", wr, zr_own, preferred_element_type=jnp.float32)
    new_tip = tip.astype(jnp.float32) - lax.psum(tip_term, "tm")

    separator = separator_diag.astype(jnp.float32)
    top = jnp.where(first, own, cross).astype(jnp.float32)
    bottom = jnp.where(first, cross.T, own).astype(jnp.float32)
    new_separator = low(separator - jnp.concatenate([top, bottom], axis=0))
    return (new_separator, arrow_fill, new_tip)


def solution(mesh):
    return jax.shard_map(
        on_device,
        mesh=mesh,
        in_specs=(
            P(("groups", "tm"), "space"),
            P(("groups", "tm"), "space"),
            P(("groups", "tm", "space"), None),
            P(("groups", "tm"), "space"),
            P("groups", "space"),
            P("groups"),
        ),
        out_specs=(
            P(("groups", "tm"), "space"),
            P(("groups", "tm"), "space"),
            P("groups", "space"),
        ),
        check_vma=False,
    )
```

time: 758 us -> 188 us (0.25)
  waiting for transfers between devices: 698 us -> 118 us
  Pallas kernels: 0 us -> 28.9 us
    all_gather x3, waiting for transfers between devices: 595 us -> 24.3 us  [the longest x1 17.4 us: on_device(): halves = lax.all_gather(interior_diag, 'space', axis=0, tiled=True)]
    ppermute x2 -> x3, waiting for transfers between devices: 72.7 us -> 39.4 us  [shifted(): return lax.ppermute(block, axis, route)]
    pallas_call x0 -> x2, Pallas kernels: none -> 28.9 us  [the longest x1 17 us: factored(): pl.pallas_call(factor_kernel, out_shape=(shape_of(n, n), shape_of(n, BLOC...]
    psum x1, waiting for transfers between devices: 29.2 us -> 52.5 us  [on_device(): new_tip = tip.astype(jnp.float32) - lax.psum(tip_term, 'tm')]
  transfers between devices with their start and end apart: 6 -> 8, of which waited for: 5 -> 6; matrix products, arithmetic and copies ran while one was open for 4% -> 9% of each run, Pallas kernels for 0% -> 9%
where the time goes in v1:
time: 188 us
  waiting for transfers between devices  118 us (63%)
  Pallas kernels  28.9 us (15%)
  between operations  13.9 us (7%)
  matrix products  12.4 us (7%)
  other arithmetic  6.04 us (3%)
  local copies, waits for them, and re-layouts  4.47 us (2%)
  starting transfers between devices  4.23 us (2%)
    psum x1, waiting for transfers between devices, on_device(): new_tip = tip.astype(jnp.float32) - lax.psum(tip_term, 'tm')  52.5 us
    ppermute x3, waiting for transfers between devices, shifted(): return lax.ppermute(block, axis, route)  39.4 us
    all_gather x1, waiting for transfers between devices, on_device(): halves = lax.all_gather(interior_diag, 'space', axis=0, tiled=True)  17.4 us
    pallas_call x1, Pallas kernels, factored(): pl.pallas_call(factor_kernel, out_shape=(shape_of(n, n), shape_of(n, BLOC...  17 us
    pallas_call x1, Pallas kernels, eliminated(): pl.pallas_call(solve_kernel, out_shape=(shape_of(n, columns), shape_of(n,...  12 us
    all_gather x1, waiting for transfers between devices, on_device(): cross = lax.all_gather(cross, 'space', axis=0, tiled=True)  6.86 us
    dot_general x1, matrix products, on_device(): jnp.einsum('kb,kc->bc', we, ze, preferred_element_type=jnp.float32)  5.51 us
    dot_general x1, matrix products, on_device(): jnp.einsum('ak,ck->ac', wr, zr_own, preferred_element_type=jnp.float32)  4.39 us
  transfers between devices with their start and end apart: 8, of which 6 were waited for; matrix products, arithmetic and copies ran while one was open for 9% of the time, Pallas kernels for 9%

profile of v1, /device:TPU:0, one launch (start us, length us, event | category | flops | bytes accessed | tf_op | source)
XLA Modules:
  0.0 187.6 jit_solution(10880313178468733773)
XLA Ops:
  7.2 0.0 copy-start.4
  7.2 0.0 all-gather.4.cloned.1.call-start
  7.2 0.7 all-gather.4.cloned.1.call-update
  7.9 0.0 all-gather.6.cloned.1.call-start
  8.0 0.7 all-gather.6.cloned.1.call-update
  8.7 0.0 all-reduce.2.cloned.1.call-start
  8.7 0.0 copy-done.4
  8.7 0.6 dynamic_slice.6.active_ref
  9.3 17.4 %all-gather.4.cloned.1.call-done.halves_ref = bf16[3072,768]{1,0:T(8,128)(2,1)} async-done(((bf16[1536,768]{1,0:T(8,128)(2,1)}), bf16[3072,768]{1,0:T(8,128)(2,1)}) %all-gather.4.cloned.1.call-update) | async-done | bytes 4718608 | tf_op jit(solution)/shard_map/all_gather | solution.py:155
  26.7 17.0 %factor.1 = (bf16[1536,1536]{1,0:T(8,128)(2,1)}, bf16[1536,256]{1,0:T(8,128)(2,1)S(1)}) custom-call(s32[1]{0:T(128)} %dynamic_slice.6.active_ref, bf16[3072,768]{1,0:T(8,128)(2,1)} %all-gather.4.cloned.1.call-done.halves_ref), custom_call_target="tpu_custom_call" | custom-call | flops 3623878656 | bytes 9437184 | tf_op jit(solution)/shard_map/factor/pallas_call | solution.py:115
  43.7 0.0 all-gather.6.cloned.1.call-done.r_ref
  43.7 12.0 %solve.1 = (bf16[1536,768]{1,0:T(8,128)(2,1)}, bf16[1536,768]{1,0:T(8,128)(2,1)}, bf16[768,1536]{1,0:T(8,128)(2,1)}, bf16[768,1536]{1,0:T(8,128)(2,1)}, bf16[768,768]{1,0:T(8,128)(2,1)S(1)}) custom-call(bf16[1536,1536]{1,0:T(8,128)(2,1)} %get-tuple-element.10.lt_ref, bf16[1536,256]{1,0:T(8,128)(2,1)S(1)} %get-tuple-element.11.p_ref, ...), custom_call_target="tpu_custom_call" | custom-call | flops 5435817984 | bytes 18874368 | tf_op jit(solution)/shard_map/solve/pallas_call | solution.py:134
  55.7 0.2 collective-permute-start.1
  55.9 4.4 %fusion.6 = f32[768,384]{1,0:T(8,128)} fusion(bf16[768,1536]{1,0:T(8,128)(2,1)} %get-tuple-element.15, bf16[768,1536]{1,0:T(8,128)(2,1)} %get-tuple-element.16, s32[]{:T(128)S(6)} %select_n.42), kind=kOutput, calls=%fused_computation.7 | convolution fusion | flops 905969664 | bytes 4718596 | tf_op jit(solution)/shard_map/ak,ck->ac/dot_general | solution.py:176
  60.3 0.0 all-reduce.2.cloned.1.call-update
  60.3 0.0 all-gather.8.cloned.1.call-start
  60.3 0.1 collective-permute-done.1
  60.4 2.5 %fusion.3 = bf16[384,768]{1,0:T(8,128)(2,1)S(1)} fusion(bf16[1536,768]{1,0:T(8,128)(2,1)S(1)} %collective-permute-done.1, bf16[1536,768]{1,0:T(8,128)(2,1)} %get-tuple-element.12, pred[]{:T(512)S(6)} %eq.3), kind=kOutput, calls=%fused_computation.5 | convolution fusion | flops 908034048 | bytes 7668736 | tf_op jit(solution)/shard_map/kb,kc->bc/dot_general | solution.py:168
  62.9 1.3 collective-permute-start.2
  64.2 1.3 collective-permute-start.3
  65.5 19.6 %collective-permute-done.2 = bf16[384,768]{1,0:T(8,128)(2,1)S(1)} collective-permute-done((bf16[384,768]{1,0:T(8,128)(2,1)S(1)}, bf16[384,768]{1,0:T(8,128)(2,1)S(1)}, u32[]{:S(2)}, u32[]{:S(2)}) %collective-permute-start.2) | collective-permute-done | bytes 589856 | tf_op jit(solution)/shard_map/ppermute | solution.py:17
  85.1 0.0 copy-start.2
  85.1 0.8 copy-done.2
  85.9 0.0 all-gather.8.cloned.1.call-update
  85.9 0.0 copy-start.3
  86.0 5.5 %convolution_convert_fusion = bf16[768,768]{1,0:T(8,128)(2,1)} fusion(bf16[1536,768]{1,0:T(8,128)(2,1)} %get-tuple-element.12, bf16[1536,768]{1,0:T(8,128)(2,1)} %get-tuple-element.13), kind=kOutput, calls=%fused_computation.4 | convolution fusion | flops 1812529152 | bytes 5898240 | tf_op jit(solution)/shard_map/kb,kc->bc/dot_general | solution.py:170
  91.5 1.3 collective-permute-start
  92.8 19.7 %collective-permute-done.3 = bf16[768,768]{1,0:T(8,128)(2,1)S(1)} collective-permute-done((bf16[768,768]{1,0:T(8,128)(2,1)S(1)}, bf16[768,768]{1,0:T(8,128)(2,1)S(1)}, u32[]{:S(2)}, u32[]{:S(2)}) %collective-permute-start.3) | collective-permute-done | bytes 1179680 | tf_op jit(solution)/shard_map/ppermute | solution.py:17
  112.5 52.5 %all-reduce.2.cloned.1.call-done = f32[768,384]{1,0:T(8,128)} async-done(((f32[768,384]{1,0:T(8,128)}), f32[768,384]{1,0:T(8,128)}) %all-reduce.2.cloned.1.call-update) | async-done | bytes 1179664 | tf_op jit(solution)/shard_map/psum | solution.py:177
  165.0 0.0 copy-done.3
  165.0 2.4 %convert_subtract_fusion = f32[768,384]{1,0:T(8,128)} fusion(f32[768,384]{1,0:T(8,128)} %all-reduce.2.cloned.1.call-done, bf16[768,384]{1,0:T(8,128)(2,1)S(1)} %copy-done.3), kind=kLoop, calls=%fused_computation.9 | loop fusion | flops 589824 | bytes 2949120 | tf_op jit(solution)/shard_map/sub | solution.py:177
  167.4 6.9 %all-gather.8.cloned.1.call-done = bf16[768,768]{1,0:T(8,128)(2,1)} async-done(((bf16[384,768]{1,0:T(8,128)(2,1)}), bf16[768,768]{1,0:T(8,128)(2,1)}) %all-gather.8.cloned.1.call-update) | async-done | bytes 1179664 | tf_op jit(solution)/shard_map/all_gather | solution.py:172
  174.3 0.0 copy-start
  174.3 1.7 copy.9
  175.9 0.0 copy-start.1
  175.9 0.0 collective-permute-done
  176.0 0.0 copy-done
  176.0 1.6 broadcast_select_fusion.1
  177.6 0.4 copy-done.1
  178.0 2.0 %subtract_convert_fusion = bf16[1536,768]{1,0:T(8,128)(2,1)} fusion(bf16[1536,768]{1,0:T(8,128)(2,1)S(1)} %copy-done.1, bf16[768,768]{1,0:T(8,128)(2,1)S(1)} %get-tuple-element.18, bf16[768,768]{1,0:T(8,128)(2,1)S(1)} %get-tuple-element.17), kind=kLoop, calls=%fused_computation | loop fusion | flops 8257536 | bytes 7077888 | tf_op jit(solution)/shard_map/convert_element_type | solution.py:21
  180.0 1.0 copy.12
Async XLA Ops:
  7.2 1.5 copy-start.4
  7.2 19.5 %all-gather.4.cloned.1.call-start = ((), (), s32[]{:S(2)}) async-start(), calls=%async_computation | async-start | bytes 7077888 | tf_op jit(solution)/shard_map/all_gather | solution.py:155
  7.9 35.8 %all-gather.6.cloned.1.call-start = ((), (), s32[]{:S(2)}) async-start(), calls=%async_computation.1 | async-start | bytes 3538944 | tf_op jit(solution)/shard_map/all_gather | solution.py:156
  8.7 156.4 %all-reduce.2.cloned.1.call-start = ((), (), s32[]{:S(2)}) async-start(), calls=%async_computation.3 | async-start | bytes 2359296 | tf_op jit(solution)/shard_map/psum | solution.py:177
  55.7 4.7 %collective-permute-start.1 = (bf16[1536,768]{1,0:T(8,128)(2,1)}, bf16[1536,768]{1,0:T(8,128)(2,1)S(1)}, u32[]{:S(2)}, u32[]{:S(2)}) collective-permute-start(bf16[1536,768]{1,0:T(8,128)(2,1)} %get-tuple-element.13), channel_id=1, source_target_pairs={{0,1},{1,0},{2,3},{3,2},{4,5},{5,4},{6,7},{7,6},{8,9},{9,8},{10,11... | collective-permute-start | bytes 7077896 | tf_op jit(solution)/shard_map/ppermute | solution.py:162
  60.3 114.0 %all-gather.8.cloned.1.call-start = ((), (), s32[]{:S(2)}) async-start(), calls=%async_computation.2 | async-start | bytes 1769472 | tf_op jit(solution)/shard_map/all_gather | solution.py:172
  62.9 22.2 %collective-permute-start.2 = (bf16[384,768]{1,0:T(8,128)(2,1)S(1)}, bf16[384,768]{1,0:T(8,128)(2,1)S(1)}, u32[]{:S(2)}, u32[]{:S(2)}) collective-permute-start(bf16[384,768]{1,0:T(8,128)(2,1)S(1)} %fusion.3), channel_id=1, source_target_pairs={{2,0},{4,2},{6,4},{8,6},{10,8},{12,10},{14,12},{3,1},{5,3},{7,5},{... | collective-permute-start | bytes 1769480 | tf_op jit(solution)/shard_map/ppermute | solution.py:17
  64.2 48.3 %collective-permute-start.3 = (bf16[768,768]{1,0:T(8,128)(2,1)S(1)}, bf16[768,768]{1,0:T(8,128)(2,1)S(1)}, u32[]{:S(2)}, u32[]{:S(2)}) collective-permute-start(bf16[768,768]{1,0:T(8,128)(2,1)S(1)} %get-tuple-element.14), channel_id=1, source_target_pairs={{2,0},{4,2},{6,4},{8,6},{10,8},{12,10},{14,12},{3,1},{5,3},{7,5},{... | collective-permute-start | bytes 3538952 | tf_op jit(solution)/shard_map/ppermute | solution.py:17
  85.1 0.8 copy-start.2
  85.9 79.1 %copy-start.3 = (bf16[768,384]{1,0:T(8,128)(2,1)S(1)}, bf16[768,384]{1,0:T(8,128)(2,1)}, u32[]{:S(2)}) copy-start(bf16[768,384]{1,0:T(8,128)(2,1)} %param.10) | copy-start | bytes 1769476
  91.5 84.5 %collective-permute-start = (bf16[768,768]{1,0:T(8,128)(2,1)}, bf16[768,768]{1,0:T(8,128)(2,1)}, u32[]{:S(2)}, u32[]{:S(2)}) collective-permute-start(bf16[768,768]{1,0:T(8,128)(2,1)} %convolution_convert_fusion), channel_id=1, source_target_pairs={{2,0},{4,2},{6,4},{8,6},{10,8},{12,10},{14,12},{3,1},{5,3},{7,5},{... | collective-permute-start | bytes 3538952 | tf_op jit(solution)/shard_map/ppermute | solution.py:17
  174.3 1.7 copy-start
  175.9 2.0 %copy-start.1 = (bf16[1536,768]{1,0:T(8,128)(2,1)S(1)}, bf16[1536,768]{1,0:T(8,128)(2,1)}, u32[]{:S(2)}) copy-start(bf16[1536,768]{1,0:T(8,128)(2,1)} %param.9) | copy-start | bytes 7077892
Sparse Core Ops, SparseCore 0:
  9.5 17.1 all-gather.3
  28.3 12.1 all-gather.5
  60.4 104.5 all-reduce.1
  166.5 7.7 all-gather.7

commit v2 on v1

--- a/solution.py
+++ b/solution.py
@@ -60,12 +60,15 @@
     return x_ref[...] * row_scale * column_scale
 
 
-def factor_kernel(active_ref, halves_ref, lt_ref, p_ref, d_ref, u_ref, x_ref):
-    n = d_ref.shape[0]
-    width = halves_ref.shape[1]
-    for half in range(n // width):
-        d_ref[:, half * width:(half + 1) * width] = halves_ref[half * n:(half + 1) * n, :]
-    keep = active_ref[0] == 2
+def factor_kernel(case_ref, own_ref, other_ref, lt_ref, p_ref, d_ref, u_ref, x_ref):
+    n, width = own_ref.shape
+    first = case_ref[1] == 0
+    for lo in range(0, n, BLOCK):
+        rows = slice(lo, lo + BLOCK)
+        own, other = own_ref[rows, :], other_ref[rows, :]
+        d_ref[rows, :width] = jnp.where(first, own, other)
+        d_ref[rows, width:] = jnp.where(first, other, own)
+    keep = case_ref[0] == 2
     for k in range(n // BLOCK):
         lo, hi = k * BLOCK, (k + 1) * BLOCK
         row = d_ref[lo:hi, lo:].astype(jnp.float32)
@@ -85,19 +88,31 @@
             lt_ref[hi:, lo:hi] = low(product(low(column), p_low))
 
 
-def solve_kernel(lt_ref, p_ref, e_ref, r_ref, we_ref, ze_ref, wr_ref, zr_ref, arrow_ref):
+def arrow_kernel(case_ref, lt_ref, p_ref, r_ref, wr_ref, tip_ref, z_ref):
+    n = lt_ref.shape[0]
+    width = tip_ref.shape[1]
+    mine = pl.ds(pl.multiple_of(case_ref[1] * width, width), width)
+    for k in range(n // BLOCK):
+        lo, hi = k * BLOCK, (k + 1) * BLOCK
+        r = r_ref[:, lo:hi]
+        if k:
+            r = low(r.astype(jnp.float32) - product(wr_ref[:, :lo], lt_ref[:lo, lo:hi]))
+        wr_ref[:, lo:hi] = r
+        z_ref[:, lo:hi] = low(product(wr_ref[mine, lo:hi], p_ref[lo:hi, :]))
+    tip_ref[...] = low(lax.dot_general(
+        wr_ref[...], z_ref[...], (((1,), (1,)), ((), ())), preferred_element_type=jnp.float32
+    ))
+
+
+def solve_kernel(lt_ref, p_ref, e_ref, wr_ref, we_ref, ze_ref, arrow_ref):
     n = lt_ref.shape[0]
     for k in range(n // BLOCK):
         lo, hi = k * BLOCK, (k + 1) * BLOCK
         e = e_ref[lo:hi, :]
-        r = r_ref[:, lo:hi]
         if k:
             e = low(e.astype(jnp.float32) - product(lt_ref[lo:hi, :lo], we_ref[:lo, :]))
-            r = low(r.astype(jnp.float32) - product(wr_ref[:, :lo], lt_ref[:lo, lo:hi]))
         we_ref[lo:hi, :] = e
-        wr_ref[:, lo:hi] = r
         ze_ref[lo:hi, :] = low(product(p_ref[lo:hi, :], e))
-        zr_ref[:, lo:hi] = low(product(r, p_ref[lo:hi, :]))
     arrow_ref[...] = low(-product(wr_ref[...], ze_ref[...]))
 
 
@@ -109,13 +124,16 @@
     return jax.ShapeDtypeStruct(dims, jnp.bfloat16)
 
 
-def factored(length, halves):
-    width = halves.shape[1]
-    n = halves.shape[0] * width // (halves.shape[0] // 2)
+def in_smem():
+    return [pl.BlockSpec(memory_space=pltpu.SMEM)]
+
+
+def factored(case, own, other):
+    n = own.shape[0]
     return pl.pallas_call(
         factor_kernel,
         out_shape=(shape_of(n, n), shape_of(n, BLOCK)),
-        in_specs=[pl.BlockSpec(memory_space=pltpu.SMEM)] + in_vmem(1),
+        in_specs=in_smem() + in_vmem(2),
         out_specs=tuple(in_vmem(2)),
         scratch_shapes=[
             pltpu.VMEM((n, n), jnp.bfloat16),
@@ -123,63 +141,89 @@
             pltpu.VMEM((BLOCK, BLOCK), jnp.float32),
         ],
         compiler_params=pltpu.CompilerParams(vmem_limit_bytes=VMEM_LIMIT),
-        cost_estimate=pl.CostEstimate(flops=n * n * n, bytes_accessed=4 * n * n, transcendentals=0),
+        cost_estimate=pl.CostEstimate(flops=5 * n * n * n, bytes_accessed=4 * n * n, transcendentals=0),
         name="factor",
-    )(length, halves)
-
-
-def eliminated(lt, p, couple, arrows):
+    )(case, own, other)
+
+
+def arrow_terms(case, lt, p, arrows, tip_width):
+    rows, n = arrows.shape
+    return pl.pallas_call(
+        arrow_kernel,
+        out_shape=(shape_of(rows, n), shape_of(rows, tip_width)),
+        in_specs=in_smem() + in_vmem(3),
+        out_specs=tuple(in_vmem(2)),
+        scratch_shapes=[pltpu.VMEM((tip_width, n), jnp.bfloat16)],
+        compiler_params=pltpu.CompilerParams(vmem_limit_bytes=VMEM_LIMIT),
+        cost_estimate=pl.CostEstimate(
+            flops=n * n * rows + 2 * n * rows * tip_width,
+            bytes_accessed=2 * (n * n + 2 * n * rows),
+            transcendentals=0,
+        ),
+        name="arrow",
+    )(case, lt, p, arrows)
+
+
+def eliminated(lt, p, couple, wr):
     n, columns = couple.shape
-    rows = arrows.shape[0]
+    rows = wr.shape[0]
     return pl.pallas_call(
         solve_kernel,
-        out_shape=(
-            shape_of(n, columns), shape_of(n, columns),
-            shape_of(rows, n), shape_of(rows, n), shape_of(rows, columns),
-        ),
+        out_shape=(shape_of(n, columns), shape_of(n, columns), shape_of(rows, columns)),
         in_specs=in_vmem(4),
-        out_specs=tuple(in_vmem(5)),
+        out_specs=tuple(in_vmem(3)),
         compiler_params=pltpu.CompilerParams(vmem_limit_bytes=VMEM_LIMIT),
         cost_estimate=pl.CostEstimate(
-            flops=n * n * (columns + rows) + 2 * n * columns * rows,
-            bytes_accessed=2 * (n * n + 3 * n * columns + 3 * n * rows),
+            flops=n * n * columns + 2 * n * columns * rows,
+            bytes_accessed=2 * (n * n + 3 * n * columns + n * rows),
             transcendentals=0,
         ),
         name="solve",
-    )(lt, p, couple, arrows)
+    )(lt, p, couple, wr)
+
+
+def swapped(block):
+    return lax.ppermute(block, "space", [(0, 1), (1, 0)])
 
 
 def on_device(interior_diag, coupling, arrow_rows, separator_diag, tip, lengths):
     position = lax.axis_index("tm")
     core = lax.axis_index("space")
-    halves = lax.all_gather(interior_diag, "space", axis=0, tiled=True)
+    first = core == 0
+    other_diag = swapped(interior_diag)
+    arrow_rows, other_diag = lax.optimization_barrier((arrow_rows, other_diag))
     arrows = lax.all_gather(arrow_rows, "space", axis=0, tiled=True)
     length = lax.dynamic_slice(lengths, (position,), (1,))
-    lt, p = factored(length, halves)
-    we, ze, wr, zr, own_arrow = eliminated(lt, p, coupling, arrows)
+    case = jnp.concatenate([length, core.astype(length.dtype)[None]])
+    lt, p = factored(case, interior_diag, other_diag)
+
+    wr, tip_term = arrow_terms(case, lt, p, arrows, tip.shape[1])
+    tip_sum = lax.psum(tip_term, "tm")
+
+    we, ze, own_arrow = eliminated(lt, p, coupling, wr)
     arrow_fill = shifted(own_arrow, "tm", -1)
-
-    other_ze = lax.ppermute(ze, "space", [(0, 1), (1, 0)])
-    first = core == 0
+    other_ze = swapped(ze)
+    own = low(jnp.einsum("kb,kc->bc", we, ze, preferred_element_type=jnp.float32))
+    own, other_ze, tip_sum = lax.optimization_barrier((own, other_ze, tip_sum))
+    own = shifted(own, "tm", -1)
+
     width = coupling.shape[1]
     part = width // 2
     left = jnp.where(first, we[:, :part], other_ze[:, part:])
     right = jnp.where(first, other_ze, we)
     cross = low(jnp.einsum("kb,kc->bc", left, right, preferred_element_type=jnp.float32))
     cross = shifted(cross, "tm", -1)
-    own = low(jnp.einsum("kb,kc->bc", we, ze, preferred_element_type=jnp.float32))
-    own = shifted(own, "tm", -1)
     cross = lax.all_gather(cross, "space", axis=0, tiled=True)
-
-    tip_width = tip.shape[1]
-    zr_own = lax.dynamic_slice(zr, (core * tip_width, 0), (tip_width, zr.shape[1]))
-    tip_term = jnp.einsum("ak,ck->ac", wr, zr_own, preferred_element_type=jnp.float32)
-    new_tip = tip.astype(jnp.float32) - lax.psum(tip_term, "tm")
-
-    separator = separator_diag.astype(jnp.float32)
-    top = jnp.where(first, own, cross).astype(jnp.float32)
-    bottom = jnp.where(first, cross.T, own).astype(jnp.float32)
-    new_separator = low(separator - jnp.concatenate([top, bottom], axis=0))
+    cross = jnp.where(first, cross.T, cross)
+
+    halves = separator_diag.reshape(2, width, width)
+    mine = lax.broadcasted_iota(jnp.int32, halves.shape, 0) == core
+    crossed = low(halves.astype(jnp.float32) - cross.astype(jnp.float32)[None])
+    crossed = jnp.where(mine, halves, crossed)
+    crossed, own = lax.optimization_barrier((crossed, own))
+    result = crossed.astype(jnp.float32) - jnp.where(mine, own.astype(jnp.float32)[None], 0.0)
+    new_separator = low(result).reshape(separator_diag.shape)
+    new_tip = tip.astype(jnp.float32) - tip_sum.astype(jnp.float32)
     return (new_separator, arrow_fill, new_tip)
 
 

time: 188 us -> 206 us (1.096)
  waiting for transfers between devices: 118 us -> 129 us
  Pallas kernels: 28.9 us -> 33.9 us
  local copies, waits for them, and re-layouts: 4.47 us -> 9.31 us
  matrix products: 12.4 us -> 7.91 us
    psum x1, waiting for transfers between devices: 52.5 us -> 70 us  [on_device(): tip_sum = lax.psum(tip_term, 'tm')]
    all_gather x1 -> x0, waiting for transfers between devices: 17.4 us -> none  [on_device(): halves = lax.all_gather(interior_diag, 'space', axis=0, tiled=True)]
    ppermute x3, waiting for transfers between devices: 39.4 us -> 54.7 us  [shifted(): return lax.ppermute(block, axis, route)]
    pallas_call x0 -> x1, Pallas kernels: none -> 9.54 us  [arrow_terms(): pl.pallas_call(arrow_kernel, out_shape=(shape_of(rows, n), shape_of(rows,...]
    all_gather x1, waiting for transfers between devices: 6.86 us -> 0.01 us  [on_device(): cross = lax.all_gather(cross, 'space', axis=0, tiled=True)]
    ppermute x1 -> x2, waiting for transfers between devices: 0.06 us -> 4.51 us  [swapped(): return lax.ppermute(block, 'space', [(0, 1), (1, 0)])]
    dot_general x1 -> x0, matrix products: 4.39 us -> none  [on_device(): jnp.einsum('ak,ck->ac', wr, zr_own, preferred_element_type=jnp.float32)]
    unnamed x11 -> x15, local copies, waits for them, and re-layouts: 2.23 us -> 6.4 us
  transfers between devices with their start and end apart: 8 -> 8, of which waited for: 6 -> 5; matrix products, arithmetic and copies ran while one was open for 9% -> 6% of each run, Pallas kernels for 9% -> 8%
where the time goes in v2:
time: 206 us
  waiting for transfers between devices  129 us (63%)
  Pallas kernels  33.9 us (16%)
  between operations  13.9 us (7%)
  local copies, waits for them, and re-layouts  9.31 us (5%)
  matrix products  7.91 us (4%)
  other arithmetic  6.88 us (3%)
  starting transfers between devices  4.87 us (2%)
    psum x1, waiting for transfers between devices, on_device(): tip_sum = lax.psum(tip_term, 'tm')  70 us
    ppermute x3, waiting for transfers between devices, shifted(): return lax.ppermute(block, axis, route)  54.7 us
    pallas_call x1, Pallas kernels, factored(): pl.pallas_call(factor_kernel, out_shape=(shape_of(n, n), shape_of(n, BLOC...  15.7 us
    pallas_call x1, Pallas kernels, arrow_terms(): pl.pallas_call(arrow_kernel, out_shape=(shape_of(rows, n), shape_of(rows,...  9.54 us
    pallas_call x1, Pallas kernels, eliminated(): pl.pallas_call(solve_kernel, out_shape=(shape_of(n, columns), shape_of(n,...  8.71 us
    unnamed x15, local copies, waits for them, and re-layouts  6.4 us
    dot_general x1, matrix products, on_device(): jnp.einsum('kb,kc->bc', we, ze, preferred_element_type=jnp.float32)  5.44 us
    ppermute x2, waiting for transfers between devices, swapped(): return lax.ppermute(block, 'space', [(0, 1), (1, 0)])  4.51 us
  transfers between devices with their start and end apart: 8, of which 5 were waited for; matrix products, arithmetic and copies ran while one was open for 6% of the time, Pallas kernels for 8%

profile of v2, /device:TPU:0, one launch (start us, length us, event | category | flops | bytes accessed | tf_op | source)
XLA Modules:
  0.0 206.0 jit_solution(6732235557175795478)
XLA Ops:
  7.2 0.0 all-gather.3.cloned.1.call-start
  7.2 0.5 collective-permute-start
  7.7 4.5 %collective-permute-done.other_ref = bf16[1536,768]{1,0:T(8,128)(2,1)} collective-permute-done((bf16[1536,768]{1,0:T(8,128)(2,1)}, bf16[1536,768]{1,0:T(8,128)(2,1)}, u32[]{:S(2)}, u32[]{:S(2)}) %collective-permute-start) | collective-permute-done | bytes 2359328 | tf_op jit(solution)/shard_map/ppermute | solution.py:186
  12.2 0.0 all-gather.3.cloned.1.call-update
  12.3 0.0 all-reduce.2.cloned.1.call-start
  12.3 1.2 dynamic_slice.3
  13.6 0.7 pad_add_fusion.case_ref
  14.3 0.0 copy-start
  14.3 1.7 copy-done
  15.9 15.7 %factor.1 = (bf16[1536,1536]{1,0:T(8,128)(2,1)}, bf16[1536,256]{1,0:T(8,128)(2,1)S(1)}) custom-call(s32[2]{0:T(128)S(1)} %pad_add_fusion.case_ref, bf16[1536,768]{1,0:T(8,128)(2,1)S(1)} %copy-done, bf16[1536,768]{1,0:T(8,128)(2,1)} %collective-permute-done.other_ref), custom_call_target="tpu_custom_call" | custom-call | flops 18119393280 | bytes 9437184 | tf_op jit(solution)/shard_map/factor/pallas_call | solution.py:133
  31.6 0.0 all-gather.3.cloned.1.call-done.r_ref
  31.6 9.5 %arrow.1 = (bf16[768,1536]{1,0:T(8,128)(2,1)S(1)}, bf16[768,384]{1,0:T(8,128)(2,1)}) custom-call(s32[2]{0:T(128)S(1)} %pad_add_fusion.case_ref, bf16[1536,1536]{1,0:T(8,128)(2,1)} %get-tuple-element.18.lt_ref, bf16[1536,256]{1,0:T(8,128)(2,1)S(1)} %get-tuple-element.19.p_ref, bf16[768,1536]{1,0:T(8,128)(2,1)} %all-gather.3.cloned.1.call-done.r_ref), custom_call_target="tpu_custom_call" | custom-call | flops 2717908992 | bytes 9437184 | tf_op jit(solution)/shard_map/arrow/pallas_call | solution.py:151
  41.2 0.0 copy-start.1
  41.2 1.4 copy-done.1
  42.6 8.7 %solve.1 = (bf16[1536,768]{1,0:T(8,128)(2,1)}, bf16[1536,768]{1,0:T(8,128)(2,1)}, bf16[768,768]{1,0:T(8,128)(2,1)S(1)}) custom-call(bf16[1536,1536]{1,0:T(8,128)(2,1)} %get-tuple-element.18.lt_ref, bf16[1536,256]{1,0:T(8,128)(2,1)S(1)} %get-tuple-element.19.p_ref, bf16[1536,768]{1,0:T(8,128)(2,1)} %e_ref.1, bf16[768,1536]{1,0:T(8,128)(2,1)} %copy-done.1), custom_call_target="tpu_custom_call" | custom-call | flops 3623878656 | bytes 14155776 | tf_op jit(solution)/shard_map/solve/pallas_call | solution.py:170
  51.3 0.4 collective-permute-start.1
  51.6 0.0 all-reduce.2.cloned.1.call-update
  51.7 0.0 all-gather.5.cloned.1.call-start
  51.7 5.4 %convolution_convert_fusion = bf16[768,768]{1,0:T(8,128)(2,1)} fusion(bf16[1536,768]{1,0:T(8,128)(2,1)} %get-tuple-element.22, bf16[1536,768]{1,0:T(8,128)(2,1)} %get-tuple-element.23), kind=kOutput, calls=%fused_computation.6 | convolution fusion | flops 1812529152 | bytes 5898240 | tf_op jit(solution)/shard_map/kb,kc->bc/dot_general | solution.py:206
  57.2 70.0 %all-reduce.2.cloned.1.call-done = bf16[768,384]{1,0:T(8,128)(2,1)} async-done(((bf16[768,384]{1,0:T(8,128)(2,1)}), bf16[768,384]{1,0:T(8,128)(2,1)}) %all-reduce.2.cloned.1.call-update) | async-done | bytes 589840 | tf_op jit(solution)/shard_map/psum | solution.py:201
  127.1 0.0 collective-permute-done.1
  127.1 2.5 %fusion.4 = bf16[384,768]{1,0:T(8,128)(2,1)S(1)} fusion(bf16[1536,768]{1,0:T(8,128)(2,1)S(1)} %collective-permute-done.1, bf16[1536,768]{1,0:T(8,128)(2,1)} %get-tuple-element.22, pred[]{:T(512)S(6)} %eq.12), kind=kOutput, calls=%fused_computation.7 | convolution fusion | flops 908034048 | bytes 7668736 | tf_op jit(solution)/shard_map/kb,kc->bc/dot_general | solution.py:214
  129.6 1.3 collective-permute-start.2
  130.9 1.3 collective-permute-start.4
  132.2 15.6 %collective-permute-done.2 = bf16[384,768]{1,0:T(8,128)(2,1)S(1)} collective-permute-done((bf16[384,768]{1,0:T(8,128)(2,1)S(1)}, bf16[384,768]{1,0:T(8,128)(2,1)S(1)}, u32[]{:S(2)}, u32[]{:S(2)}) %collective-permute-start.2) | collective-permute-done | bytes 589856 | tf_op jit(solution)/shard_map/ppermute | solution.py:17
  147.8 0.0 copy-start.6
  147.8 0.8 copy-done.6
  148.6 0.0 all-gather.5.cloned.1.call-update
  148.6 1.3 collective-permute-start.3
  149.9 23.1 %collective-permute-done.4 = bf16[768,768]{1,0:T(8,128)(2,1)S(1)} collective-permute-done((bf16[768,768]{1,0:T(8,128)(2,1)S(1)}, bf16[768,768]{1,0:T(8,128)(2,1)S(1)}, u32[]{:S(2)}, u32[]{:S(2)}) %collective-permute-start.4) | collective-permute-done | bytes 1179680 | tf_op jit(solution)/shard_map/ppermute | solution.py:17
  173.0 0.0 copy-start.4
  173.0 2.8 %convert_subtract_fusion = f32[768,384]{1,0:T(8,128)} fusion(bf16[768,384]{1,0:T(8,128)(2,1)} %all-reduce.2.cloned.1.call-done, bf16[768,384]{1,0:T(8,128)(2,1)} %param.10), kind=kLoop, calls=%fused_computation.10 | loop fusion | flops 884736 | bytes 2359296 | tf_op jit(solution)/shard_map/sub | solution.py:226
  175.8 0.0 copy-done.4
  175.8 0.0 all-gather.5.cloned.1.call-done
  175.8 0.0 copy-start.2
  175.8 1.7 copy.9
  177.5 0.0 copy-done.2
  177.5 0.0 copy-start.3
  177.5 0.2 fusion.7
  177.7 1.5 copy-done.3
  179.2 0.9 fusion
  180.1 16.1 %collective-permute-done.3 = bf16[768,768]{1,0:T(8,128)(2,1)S(1)} collective-permute-done((bf16[768,768]{1,0:T(8,128)(2,1)}, bf16[768,768]{1,0:T(8,128)(2,1)S(1)}, u32[]{:S(2)}, u32[]{:S(2)}) %collective-permute-start.3) | collective-permute-done | bytes 1179680 | tf_op jit(solution)/shard_map/ppermute | solution.py:17
  196.1 0.2 convert_element_type.36
  196.3 0.0 copy-start.5
  196.3 2.2 %subtract_convert_fusion = bf16[2,768,768]{2,1,0:T(8,128)(2,1)} fusion(bf16[2,768,768]{2,1,0:T(8,128)(2,1)S(1)} %fusion, f32[768,768]{1,0:T(8,128)S(1)} %convert_element_type.36, pred[2]{0:T(512)(128)(4,1)S(1)} %iota_compare_fusion), kind=kLoop, calls=%fused_computation | loop fusion | flops 4718592 | bytes 7077890 | tf_op jit(solution)/shard_map/convert_element_type | solution.py:21
  198.5 0.0 copy-done.5
  198.5 1.0 copy.12
  (1 shorter events, 0.0 us)
Async XLA Ops:
  7.2 24.5 %all-gather.3.cloned.1.call-start = ((), (), s32[]{:S(2)}) async-start(), calls=%async_computation | async-start | bytes 3538944 | tf_op jit(solution)/shard_map/all_gather | solution.py:195
  7.2 5.0 %collective-permute-start = (bf16[1536,768]{1,0:T(8,128)(2,1)}, bf16[1536,768]{1,0:T(8,128)(2,1)}, u32[]{:S(2)}, u32[]{:S(2)}) collective-permute-start(bf16[1536,768]{1,0:T(8,128)(2,1)} %own_ref.1), channel_id=1, source_target_pairs={{0,1},{1,0},{2,3},{3,2},{4,5},{5,4},{6,7},{7,6},{8,9},{9,8},{10,11... | collective-permute-start | bytes 7077896 | tf_op jit(solution)/shard_map/ppermute | solution.py:186
  12.3 114.9 %all-reduce.2.cloned.1.call-start = ((), (), s32[]{:S(2)}) async-start(), calls=%async_computation.1 | async-start | bytes 1179648 | tf_op jit(solution)/shard_map/psum | solution.py:201
  14.3 1.7 copy-start
  41.2 1.4 copy-start.1
  51.3 75.9 %collective-permute-start.1 = (bf16[1536,768]{1,0:T(8,128)(2,1)}, bf16[1536,768]{1,0:T(8,128)(2,1)S(1)}, u32[]{:S(2)}, u32[]{:S(2)}) collective-permute-start(bf16[1536,768]{1,0:T(8,128)(2,1)} %get-tuple-element.23), channel_id=1, source_target_pairs={{0,1},{1,0},{2,3},{3,2},{4,5},{5,4},{6,7},{7,6},{8,9},{9,8},{10,11... | collective-permute-start | bytes 7077896 | tf_op jit(solution)/shard_map/ppermute | solution.py:186
  51.7 124.2 %all-gather.5.cloned.1.call-start = ((), (), s32[]{:S(2)}) async-start(), calls=%async_computation.2 | async-start | bytes 1769472 | tf_op jit(solution)/shard_map/all_gather | solution.py:216
  129.6 18.2 %collective-permute-start.2 = (bf16[384,768]{1,0:T(8,128)(2,1)S(1)}, bf16[384,768]{1,0:T(8,128)(2,1)S(1)}, u32[]{:S(2)}, u32[]{:S(2)}) collective-permute-start(bf16[384,768]{1,0:T(8,128)(2,1)S(1)} %fusion.4), channel_id=1, source_target_pairs={{2,0},{4,2},{6,4},{8,6},{10,8},{12,10},{14,12},{3,1},{5,3},{7,5},{... | collective-permute-start | bytes 1769480 | tf_op jit(solution)/shard_map/ppermute | solution.py:17
  130.9 42.1 %collective-permute-start.4 = (bf16[768,768]{1,0:T(8,128)(2,1)S(1)}, bf16[768,768]{1,0:T(8,128)(2,1)S(1)}, u32[]{:S(2)}, u32[]{:S(2)}) collective-permute-start(bf16[768,768]{1,0:T(8,128)(2,1)S(1)} %get-tuple-element.29), channel_id=1, source_target_pairs={{2,0},{4,2},{6,4},{8,6},{10,8},{12,10},{14,12},{3,1},{5,3},{7,5},{... | collective-permute-start | bytes 3538952 | tf_op jit(solution)/shard_map/ppermute | solution.py:17
  147.8 0.8 copy-start.6
  148.6 47.5 %collective-permute-start.3 = (bf16[768,768]{1,0:T(8,128)(2,1)}, bf16[768,768]{1,0:T(8,128)(2,1)S(1)}, u32[]{:S(2)}, u32[]{:S(2)}) collective-permute-start(bf16[768,768]{1,0:T(8,128)(2,1)} %convolution_convert_fusion), channel_id=1, source_target_pairs={{2,0},{4,2},{6,4},{8,6},{10,8},{12,10},{14,12},{3,1},{5,3},{7,5},{... | collective-permute-start | bytes 3538952 | tf_op jit(solution)/shard_map/ppermute | solution.py:17
  173.0 2.8 %copy-start.4 = (bf16[768,768]{1,0:T(8,128)(2,1)}, bf16[768,768]{1,0:T(8,128)(2,1)S(1)}, u32[]{:S(2)}) copy-start(bf16[768,768]{1,0:T(8,128)(2,1)S(1)} %collective-permute-done.4) | copy-start | bytes 3538948
  175.8 1.7 copy-start.2
  177.5 1.7 copy-start.3
  196.3 2.2 %copy-start.5 = (bf16[768,768]{1,0:T(8,128)(2,1)S(1)}, bf16[768,768]{1,0:T(8,128)(2,1)}, u32[]{:S(2)}) copy-start(bf16[768,768]{1,0:T(8,128)(2,1)} %copy-done.4) | copy-start | bytes 3538948
Sparse Core Ops, SparseCore 0:
  12.4 13.5 all-gather.2
  51.8 75.3 all-reduce.1
  148.7 9.0 all-gather.4
